TPU v7x, 128 devices: a whole 4x4x4 slice. The times are simulated.
128 devices in a mesh: dp: 32 (over z, y, x_hi), tensor: 4 (over x_lo, core).
Axes of the slice: x: 4 (x_hi: 2, x_lo: 2; x = x_hi * 2 + x_lo), y: 4, z: 4, core: 2. Of those that a mesh axis runs over, the one named last changes fastest.
Arguments:
- kv_weight: bfloat16 [32, 512, 16384], P(None, 'dp', 'tensor'), may hold values from -1.5 to 1.5
- momentum: bfloat16 [32, 512, 16384], P(None, 'dp', 'tensor'), may hold values from -36 to 36, as said below
- gradient: bfloat16 [32, 512, 16384], P(None, 'dp', 'tensor'), may hold values from -36 to 36, as said below
- head_counts: int32 [32], replicated, may hold values from 16 to 64, as said below
- logit_peaks: float32 [32, 32, 64], P(None, 'dp', 'tensor'), may hold values from 1.5 to 300, as said below
Outputs:
- update: bfloat16 [32, 512, 16384], P(None, 'dp', 'tensor')
- new_weight: bfloat16 [32, 512, 16384], P(None, 'dp', 'tensor')
- new_momentum: bfloat16 [32, 512, 16384], P(None, 'dp', 'tensor')
Inputs may be any that keep to these rules, and one draw needn't show every extreme that they name: momentum: a normal or uniform draw times a row scale and a column scale. gradient: drawn like momentum. `head_counts`: heads 0 to count - 1 of a layer are kept, the others pruned; some layer keeps all 64. `logit_peaks`: positive.
All inputs are finite; a program needn't handle non-finite values.
Results may differ from a plain program's by a relative error of at most 0.015.
The roundings to bfloat16 on the way count: a program that leaves them out, or rounds other values in their place, can miss the bound.
Values may be sent and summed in bfloat16 or wider, within the bound.
No kernel may reach another device: no remote copies, remote signals or barrier semaphores. Data moves between devices by JAX's collectives and lax.ppermute only.
A program may use at most 128 MiB of HBM per device.

v0:
```python
import math

import jax
import jax.numpy as jnp
from jax import lax
from jax.sharding import PartitionSpec as P

LATENT = 512
KEY_DIM = 128
VALUE_DIM = 128
ITERS = 5
KV_OUT = 16384


momentum_decay = 0.95
first_coef = 3.4445
second_coef = -4.775
third_coef = 2.0315
epsilon = 1e-07
clip_limit = 100.0
learn_rate = 0.02
weight_decay = 0.1


def orthogonalize(current):
    norm_scale = None
    for iteration in range(ITERS):
        local_gram = lax.dot_general(
            current, current, (((1,), (1,)), ((), ())), preferred_element_type=jnp.float32
        )
        gram_matrix = lax.psum(local_gram, "tensor")
        if iteration == 0:
            norm_scale = 1.0 / (jnp.sqrt(jnp.trace(gram_matrix)) + epsilon)
            gram_matrix = gram_matrix * norm_scale * norm_scale
        square = jnp.dot(gram_matrix, gram_matrix, precision=lax.Precision.HIGHEST)
        polynomial = (second_coef * gram_matrix + third_coef * square).astype(jnp.bfloat16)
        product = jnp.dot(polynomial, current, preferred_element_type=jnp.float32)
        combined = first_coef * current.astype(jnp.float32) + product
        if iteration == 0:
            combined = combined * norm_scale
        current = combined.astype(jnp.bfloat16)
    return current


def scaled_update(owned):
    update_scale = 0.2 * math.sqrt(max(LATENT, KV_OUT))
    return (update_scale * orthogonalize(owned).astype(jnp.float32)).astype(jnp.bfloat16)


def apply_step(weight_rows, update_rows, col_factor):
    stepped = weight_rows.astype(jnp.float32) * (
        1.0 - learn_rate * weight_decay
    ) - learn_rate * update_rows.astype(jnp.float32)
    return (col_factor * stepped).astype(jnp.bfloat16)


def on_device(kv_weight, momentum, gradient, head_counts, logit_peaks):
    shard_width = momentum.shape[2]
    head_width = KEY_DIM + VALUE_DIM
    heads_here = shard_width // head_width
    first_head = lax.axis_index("tensor") * heads_here
    head_of = first_head + jnp.arange(shard_width) // head_width
    live_mask = (head_of[None, :] < head_counts[:, None]).astype(jnp.float32)
    new_momentum = (
        live_mask[:, None, :]
        * (momentum_decay * momentum.astype(jnp.float32) + gradient.astype(jnp.float32))
    ).astype(jnp.bfloat16)
    head_peak = lax.pmax(logit_peaks, "dp")
    clip_gamma = jnp.minimum(1.0, clip_limit / head_peak[:, 0, :])
    key_column = jnp.arange(shard_width) % head_width < KEY_DIM
    col_factor = jnp.where(
        key_column[None, :], jnp.sqrt(jnp.repeat(clip_gamma, head_width, axis=1)), 1.0
    )
    owned_moment = lax.all_to_all(new_momentum, "dp", split_axis=0, concat_axis=1, tiled=True)
    owned_update = scaled_update(owned_moment[0])
    update = lax.all_to_all(owned_update[None], "dp", split_axis=1, concat_axis=0, tiled=True)
    new_weight = apply_step(kv_weight, update, col_factor[:, None, :])
    return (update, new_weight, new_momentum)


def solution(mesh):
    placed = (
        P(None, "dp", "tensor"),
        P(None, "dp", "tensor"),
        P(None, "dp", "tensor"),
        P(),
        P(None, "dp", "tensor"),
    )
    return jax.shard_map(
        on_device,
        mesh=mesh,
        in_specs=placed,
        out_specs=(P(None, "dp", "tensor"), P(None, "dp", "tensor"), P(None, "dp", "tensor")),
        check_vma=False,
    )
```

profile of v0, /device:TPU:0, one launch (start us, length us, event | category | flops | bytes accessed | tf_op | source)
XLA Modules:
  0.0 614.1 jit_solution(13744515763006332075)
XLA Ops:
  8.0 4.4 multiply_convert_fusion.3
  12.4 63.7 %all_to_all.21 = bf16[32,16,4096]{2,1,0:T(8,128)(2,1)S(1)} all-to-all(bf16[32,16,4096]{2,1,0:T(8,128)(2,1)S(1)} %multiply_convert_fusion.3), channel_id=1, replica_groups=mesh['dp'=32,'tensor'=4] {'dp'}, dimensions={0} | all-to-all | bytes 8388608 | tf_op jit(solution)/shard_map/all_to_all | solution.py:74
  81.5 36.9 %all-reduce.6.cloned.1.call-done = f32[512,512]{1,0:T(8,128)} async-done(((f32[512,512]{1,0:T(8,128)}), f32[512,512]{1,0:T(8,128)}) %all-reduce.6.cloned.1.call-update) | async-done | bytes 1048592 | tf_op jit(solution)/shard_map/psum | solution.py:31
  121.0 4.1 fusion.6
  125.1 5.9 multiply_convert_fusion.2
  136.9 42.0 %all-reduce.8.cloned.1.call-done = f32[512,512]{1,0:T(8,128)} async-done(((f32[512,512]{1,0:T(8,128)}), f32[512,512]{1,0:T(8,128)}) %all-reduce.8.cloned.1.call-update) | async-done | bytes 1048592 | tf_op jit(solution)/shard_map/psum | solution.py:31
  178.8 3.9 fusion.7
  182.8 5.8 add_convert_fusion.3
  194.0 42.4 %all-reduce.10.cloned.1.call-done = f32[512,512]{1,0:T(8,128)} async-done(((f32[512,512]{1,0:T(8,128)}), f32[512,512]{1,0:T(8,128)}) %all-reduce.10.cloned.1.call-update) | async-done | bytes 1048592 | tf_op jit(solution)/shard_map/psum | solution.py:31
  236.5 3.9 fusion.8
  240.4 5.8 add_convert_fusion.2
  251.8 42.2 %all-reduce.12.cloned.1.call-done = f32[512,512]{1,0:T(8,128)} async-done(((f32[512,512]{1,0:T(8,128)}), f32[512,512]{1,0:T(8,128)}) %all-reduce.12.cloned.1.call-update) | async-done | bytes 1048592 | tf_op jit(solution)/shard_map/psum | solution.py:31
  294.1 3.9 fusion.9
  298.0 5.8 add_convert_fusion.1
  309.2 42.5 %all-reduce.14.cloned.1.call-done = f32[512,512]{1,0:T(8,128)} async-done(((f32[512,512]{1,0:T(8,128)}), f32[512,512]{1,0:T(8,128)}) %all-reduce.14.cloned.1.call-update) | async-done | bytes 1048592 | tf_op jit(solution)/shard_map/psum | solution.py:31
  351.7 3.9 fusion.10
  355.6 6.0 fusion
  361.6 22.3 %copy.16 = bf16[1,512,4096]{2,0,1:T(2,128)(2,1)} copy(bf16[1,512,4096]{2,1,0:T(8,128)(2,1)S(1)} %fusion) | data formatting | bytes 8388608 | tf_op jit(solution)/shard_map/broadcast_in_dim | solution.py:76
  384.5 27.5 %reduce = bf16[512,4096]{1,0:T(8,128)(2,1)} reduce(bf16[512,1,4096]{2,1,0:T(2,128)(2,1)} %bitcast.40, bf16[]{:T(256)} %broadcast.117), dimensions={1}, to_apply=%bitcast.39.reduce_sub_computation | reduce | bytes 8388610
  411.9 7.8 %reshape.85 = bf16[32,2,32768]{2,1,0:T(2,128)(2,1)} reshape(bf16[512,4096]{1,0:T(8,128)(2,1)} %reduce) | data formatting | bytes 8388608
  419.7 9.6 %all-to-all-start.1 = ((bf16[32,2,32768]{2,1,0:T(2,128)(2,1)}), bf16[32,2,32768]{2,1,0:T(2,128)(2,1)}, u32[]{:S(2)}, u32[]{:S(2)}) async-start(bf16[32,2,32768]{2,1,0:T(2,128)(2,1)} %reshape.85), calls=%async_computation.1 | async-start | bytes 8388608 | tf_op jit(solution)/shard_map/all_to_all | solution.py:76
  429.4 145.9 %pmax.7 = f32[32,1,16]{0,2,1:T(8,128)S(1)} all-reduce(f32[32,1,16]{0,2,1:T(8,128)S(1)} %copy-done.4), channel_id=1, replica_groups=mesh['dp'=32,'tensor'=4] {'dp'}, use_global_device_ids=true, to_apply=%region_6.7 | all-reduce | flops 512 | bytes 4096 | tf_op jit(solution)/shard_map/pmax | solution.py:68
  575.9 19.8 %reshape.86 = bf16[512,1,4096]{2,1,0:T(2,128)(2,1)} reshape(bf16[32,2,32768]{2,1,0:T(2,128)(2,1)} %all-to-all-done.1) | data formatting | bytes 8388608
  595.7 8.3 %copy.13 = bf16[1,512,4096]{2,1,0:T(8,128)(2,1)S(1)} copy(bf16[1,512,4096]{2,0,1:T(2,128)(2,1)} %bitcast.41) | data formatting | bytes 8388608
  (45 shorter events, 34.7 us)
Async XLA Ops:
  7.2 111.2 %all-reduce.6.cloned.1.call-start = ((), (), s32[]{:S(2)}) async-start(), calls=%async_computation.2 | async-start | bytes 2097152 | tf_op jit(solution)/shard_map/psum | solution.py:31
  12.4 63.7 %copy-start.1 = (bf16[32,16,4096]{2,1,0:T(8,128)(2,1)}, bf16[32,16,4096]{2,1,0:T(8,128)(2,1)S(1)}, u32[]{:S(2)}) copy-start(bf16[32,16,4096]{2,1,0:T(8,128)(2,1)S(1)} %multiply_convert_fusion.3) | copy-start | bytes 12582916
  76.1 2.0 copy-start.3
  81.5 97.4 %all-reduce.8.cloned.1.call-start = ((), (), s32[]{:S(2)}) async-start(), calls=%async_computation.3 | async-start | bytes 2097152 | tf_op jit(solution)/shard_map/psum | solution.py:31
  131.0 2.0 copy-start.5
  136.4 100.1 %all-reduce.10.cloned.1.call-start = ((), (), s32[]{:S(2)}) async-start(), calls=%async_computation.4 | async-start | bytes 2097152 | tf_op jit(solution)/shard_map/psum | solution.py:31
  188.6 2.0 copy-start.6
  194.0 100.1 %all-reduce.12.cloned.1.call-start = ((), (), s32[]{:S(2)}) async-start(), calls=%async_computation.5 | async-start | bytes 2097152 | tf_op jit(solution)/shard_map/psum | solution.py:31
  246.2 2.0 copy-start.7
  251.6 100.1 %all-reduce.14.cloned.1.call-start = ((), (), s32[]{:S(2)}) async-start(), calls=%async_computation.6 | async-start | bytes 2097152 | tf_op jit(solution)/shard_map/psum | solution.py:31
  303.9 2.0 copy-start.8
  419.7 9.6 %copy-start.4 = (f32[32,1,16]{0,2,1:T(8,128)S(1)}, f32[32,1,16]{0,2,1:T(8,128)}, u32[]{:S(2)}) copy-start(f32[32,1,16]{0,2,1:T(8,128)} %param.9) | copy-start | bytes 6148
  419.7 156.2 %all-to-all-start.1 = ((bf16[32,2,32768]{2,1,0:T(2,128)(2,1)}), bf16[32,2,32768]{2,1,0:T(2,128)(2,1)}, u32[]{:S(2)}, u32[]{:S(2)}) async-start(bf16[32,2,32768]{2,1,0:T(2,128)(2,1)} %reshape.85), calls=%async_computation.1 | async-start | bytes 8388608 | tf_op jit(solution)/shard_map/all_to_all | solution.py:76
  595.7 8.3 %copy-start.2 = (bf16[32,16,4096]{2,1,0:T(8,128)(2,1)S(1)}, bf16[32,16,4096]{2,1,0:T(8,128)(2,1)}, u32[]{:S(2)}) copy-start(bf16[32,16,4096]{2,1,0:T(8,128)(2,1)} %param.5) | copy-start | bytes 12582916
  604.0 3.3 copy-start
Sparse Core Ops, SparseCore 0:
  81.6 36.7 all-reduce.5
  136.5 42.3 all-reduce.7
  194.1 42.2 all-reduce.9
  251.7 42.2 all-reduce.11
  309.3 42.2 all-reduce.13
where the time goes:
time: 622 us; the launch traced here: 614 us
  blocking collectives  210 us (34%)
  waiting for transfers between devices  206 us (33%)
  local copies, waits for them, and re-layouts  69.3 us (11%)
  matrix products  65.8 us (11%)
  other arithmetic  37.9 us (6%)
  between operations  15 us (2%)
  starting transfers between devices  10.5 us (2%)
    psum x5, waiting for transfers between devices, orthogonalize(): gram_matrix = lax.psum(local_gram, 'tensor')  206 us
    pmax x1, blocking collectives, on_device(): head_peak = lax.pmax(logit_peaks, 'dp')  146 us
    all_to_all x1, blocking collectives, on_device(): lax.all_to_all(new_momentum, 'dp', split_axis=0, concat_axis=1, tiled=True)  63.7 us
    unnamed x23, local copies, waits for them, and re-layouts  46.7 us
    dot_general x5, matrix products, orthogonalize(): product = jnp.dot(polynomial, current, preferred_element_type=jnp.float32)  29.3 us
    unnamed x1, other arithmetic  27.5 us
    broadcast_in_dim x1, local copies, waits for them, and re-layouts, on_device(): owned_update[None]  22.3 us
    dot_general x5, matrix products, orthogonalize(): square = jnp.dot(gram_matrix, gram_matrix, precision=lax.Precision.HIGHEST)  19.8 us
  transfers between devices with their start and end apart: 6, of which 5 were waited for; matrix products, arithmetic and copies ran while one was open for 0% of the time, Pallas kernels for 0%

commit v1 on v0

v1 whole, which is shorter than its diff:
```python
import math

import jax
import jax.numpy as jnp
from jax import lax
from jax.experimental import pallas as pl
from jax.experimental.pallas import tpu as pltpu
from jax.sharding import PartitionSpec as P

LATENT = 512
KEY_DIM = 128
VALUE_DIM = 128
ITERS = 5
KV_OUT = 16384


momentum_decay = 0.95
first_coef = 3.4445
second_coef = -4.775
third_coef = 2.0315
epsilon = 1e-07
clip_limit = 100.0
learn_rate = 0.02
weight_decay = 0.1

f32 = jnp.float32
bf16 = jnp.bfloat16


def split_two(value):
    high = value.astype(bf16)
    return high, (value - high.astype(f32)).astype(bf16)


def dot(left, right):
    return jnp.dot(left, right, preferred_element_type=f32)


def polynomial_kernel(gram_ref, out_ref):
    gram = gram_ref[...]
    size = gram.shape[0]
    row = lax.broadcasted_iota(jnp.int32, (size, size), 0)
    col = lax.broadcasted_iota(jnp.int32, (size, size), 1)
    diagonal = row == col
    trace = jnp.sum(jnp.where(diagonal, gram, 0.0))
    scale = 1.0 / (jnp.sqrt(trace) + epsilon)
    gram = gram * scale * scale
    total = None
    for iteration in range(ITERS):
        high, low = split_two(gram)
        square = dot(high, high) + (dot(high, low) + dot(low, high))
        poly = (second_coef * gram + third_coef * square).astype(bf16)
        if iteration == 0:
            total = jnp.where(diagonal, first_coef, 0.0) + poly.astype(f32)
        else:
            t_high, t_low = split_two(total)
            total = first_coef * total + (dot(poly, t_high) + dot(poly, t_low))
        if iteration < ITERS - 1:
            half = first_coef * gram + (dot(poly, high) + dot(poly, low))
            h_high, h_low = split_two(half)
            gram = first_coef * half + (dot(h_high, poly) + dot(h_low, poly))
    out_ref[...] = (total * scale).astype(bf16)


def polynomial(gram):
    return pl.pallas_call(
        polynomial_kernel,
        out_shape=jax.ShapeDtypeStruct(gram.shape, bf16),
        in_specs=[pl.BlockSpec(memory_space=pltpu.VMEM)],
        out_specs=pl.BlockSpec(memory_space=pltpu.VMEM),
        compiler_params=pltpu.CompilerParams(vmem_limit_bytes=40 * 2**20),
        cost_estimate=pl.CostEstimate(
            flops=40 * 2 * gram.shape[0] ** 3, bytes_accessed=3 * 2**19, transcendentals=0
        ),
    )(gram)


def scaled_update(owned):
    update_scale = 0.2 * math.sqrt(max(LATENT, KV_OUT))
    local_gram = lax.dot_general(
        owned, owned, (((1,), (1,)), ((), ())), preferred_element_type=f32
    )
    factors = polynomial(lax.psum(local_gram, "tensor"))
    ortho = dot(factors, owned).astype(bf16)
    return (update_scale * ortho.astype(f32)).astype(bf16)


def apply_step(weight_rows, update_rows, col_factor):
    stepped = weight_rows.astype(f32) * (
        1.0 - learn_rate * weight_decay
    ) - learn_rate * update_rows.astype(f32)
    return (col_factor * stepped).astype(bf16)


def on_device(kv_weight, momentum, gradient, head_counts, logit_peaks):
    layers, rows, shard_width = momentum.shape
    head_width = KEY_DIM + VALUE_DIM
    heads_here = shard_width // head_width
    first_head = lax.axis_index("tensor") * heads_here
    head_of = first_head + jnp.arange(shard_width) // head_width
    live_mask = (head_of[None, :] < head_counts[:, None]).astype(f32)
    new_momentum = (
        live_mask[:, None, :]
        * (momentum_decay * momentum.astype(f32) + gradient.astype(f32))
    ).astype(bf16)
    head_peak = jnp.max(lax.all_gather(logit_peaks[:, 0, :], "dp"), axis=0)
    clip_gamma = jnp.minimum(1.0, clip_limit / head_peak)
    key_column = jnp.arange(shard_width) % head_width < KEY_DIM
    col_factor = jnp.where(
        key_column[None, :], jnp.sqrt(jnp.repeat(clip_gamma, head_width, axis=1)), 1.0
    )
    owned = lax.all_to_all(new_momentum, "dp", split_axis=0, concat_axis=0, tiled=True)
    owned_update = scaled_update(owned.reshape(layers * rows, shard_width))
    update = lax.all_to_all(
        owned_update.reshape(layers, rows, shard_width),
        "dp",
        split_axis=0,
        concat_axis=0,
        tiled=True,
    )
    new_weight = apply_step(kv_weight, update, col_factor[:, None, :])
    return (update, new_weight, new_momentum)


def solution(mesh):
    placed = (
        P(None, "dp", "tensor"),
        P(None, "dp", "tensor"),
        P(None, "dp", "tensor"),
        P(),
        P(None, "dp", "tensor"),
    )
    return jax.shard_map(
        on_device,
        mesh=mesh,
        in_specs=placed,
        out_specs=(P(None, "dp", "tensor"), P(None, "dp", "tensor"), P(None, "dp", "tensor")),
        check_vma=False,
    )
```

time: 622 us -> 312 us (0.50); the launches traced: 614 us -> 312 us
  waiting for transfers between devices: 206 us -> 36.9 us
  local copies, waits for them, and re-layouts: 69.3 us -> 8.61 us
  matrix products: 65.8 us -> 7.71 us
  other arithmetic: 37.9 us -> 11 us
  Pallas kernels: 0 us -> 11.6 us
    psum x5 -> x1, waiting for transfers between devices: 206 us -> 36.9 us  [scaled_update(): factors = polynomial(lax.psum(local_gram, 'tensor'))]
    all_gather x0 -> x1, blocking collectives: none -> 148 us  [on_device(): head_peak = jnp.max(lax.all_gather(logit_peaks[:, 0, :], 'dp'), axis=0)]
    pmax x1 -> x0, blocking collectives: 146 us -> none  [on_device(): head_peak = lax.pmax(logit_peaks, 'dp')]
    dot_general x15 -> x2, matrix products: 65.8 us -> 7.71 us  [the longest x1 4.38 us: dot(): return jnp.dot(left, right, preferred_element_type=f32)]
    unnamed x23 -> x14, local copies, waits for them, and re-layouts: 46.7 us -> 8.4 us
    unnamed x1 -> x0, other arithmetic: 27.5 us -> none
    broadcast_in_dim x1 -> x0, local copies, waits for them, and re-layouts: 22.3 us -> none  [on_device(): owned_update[None]]
    pallas_call x0 -> x1, Pallas kernels: none -> 11.6 us  [polynomial(): pl.pallas_call(polynomial_kernel, out_shape=jax.ShapeDtypeStruct(gram.sha...]
  transfers between devices with their start and end apart: 6 -> 2, of which waited for: 5 -> 1; matrix products, arithmetic and copies ran while one was open for 0% -> 0% of each run, Pallas kernels for 0% -> 0%
where the time goes in v1:
time: 312 us
  blocking collectives  212 us (68%)
  waiting for transfers between devices  36.9 us (12%)
  between operations  14.1 us (5%)
  Pallas kernels  11.6 us (4%)
  other arithmetic  11 us (4%)
  starting transfers between devices  9.87 us (3%)
  local copies, waits for them, and re-layouts  8.61 us (3%)
  matrix products  7.71 us (2%)
    all_gather x1, blocking collectives, on_device(): head_peak = jnp.max(lax.all_gather(logit_peaks[:, 0, :], 'dp'), axis=0)  148 us
    all_to_all x1, blocking collectives, on_device(): lax.all_to_all(new_momentum, 'dp', split_axis=0, concat_axis=0, tiled=True)  63.7 us
    psum x1, waiting for transfers between devices, scaled_update(): factors = polynomial(lax.psum(local_gram, 'tensor'))  36.9 us
    pallas_call x1, Pallas kernels, polynomial(): pl.pallas_call(polynomial_kernel, out_shape=jax.ShapeDtypeStruct(gram.sha...  11.6 us
    all_to_all x1, starting transfers between devices, on_device(): lax.all_to_all(owned_update.reshape(layers, rows, shard_width), 'dp', spl...  9.83 us
    unnamed x14, local copies, waits for them, and re-layouts  8.4 us
  transfers between devices with their start and end apart: 2, of which 1 were waited for; matrix products, arithmetic and copies ran while one was open for 0% of the time, Pallas kernels for 0%

profile of v1, /device:TPU:0, one launch (start us, length us, event | category | flops | bytes accessed | tf_op | source)
XLA Modules:
  0.0 311.6 jit_solution(6073641524945520509)
XLA Ops:
  7.2 0.0 all-reduce.2.cloned.1.call-start
  7.2 0.8 compare_convert_fusion
  8.0 4.4 %multiply_convert_fusion.2 = bf16[32,16,4096]{2,1,0:T(8,128)(2,1)S(1)} fusion(bf16[32,16,4096]{2,1,0:T(8,128)(2,1)} %param.7, bf16[32,16,4096]{2,1,0:T(8,128)(2,1)} %param.6, f32[32,4096]{1,0:T(8,128)S(1)} %compare_convert_fusion), kind=kLoop, calls=%fused_computation.2 | loop fusion | flops 12582912 | bytes 13107200 | tf_op jit(solution)/shard_map/convert_element_type | solution.py:105
  12.4 0.0 copy-start.1
  12.4 63.7 %all_to_all.10 = bf16[32,16,4096]{2,1,0:T(8,128)(2,1)S(1)} all-to-all(bf16[32,16,4096]{2,1,0:T(8,128)(2,1)S(1)} %multiply_convert_fusion.2), channel_id=1, replica_groups=mesh['dp'=32,'tensor'=4] {'dp'}, dimensions={0} | all-to-all | bytes 8388608 | tf_op jit(solution)/shard_map/all_to_all | solution.py:112
  76.1 2.0 copy-done.2
  78.1 3.3 %fusion.9 = f32[512,512]{1,0:T(8,128)} fusion(bf16[512,4096]{1,0:T(8,128)(2,1)S(1)} %bitcast.12), kind=kOutput, calls=%fused_computation.21 | convolution fusion | flops 2147483648 | bytes 5242880 | tf_op jit(solution)/shard_map/dot_general | solution.py:80
  81.5 0.0 all-reduce.2.cloned.1.call-update
  81.5 36.9 %all-reduce.2.cloned.1.call-done.gram_ref = f32[512,512]{1,0:T(8,128)} async-done(((f32[512,512]{1,0:T(8,128)}), f32[512,512]{1,0:T(8,128)}) %all-reduce.2.cloned.1.call-update) | async-done | bytes 1048592 | tf_op jit(solution)/shard_map/psum | solution.py:83
  118.4 1.2 copy-done
  119.6 11.6 %shard_map.76 = bf16[512,512]{1,0:T(8,128)(2,1)S(1)} custom-call(f32[512,512]{1,0:T(8,128)S(1)} %copy-done), custom_call_target="tpu_custom_call" | custom-call | flops 10737418240 | bytes 1572864 | tf_op jit(solution)/shard_map/pallas_call | solution.py:66
  131.2 0.0 copy-done.3
  131.2 4.4 %multiply_convert_fusion.1 = bf16[512,4096]{1,0:T(8,128)(2,1)} fusion(bf16[512,512]{1,0:T(8,128)(2,1)S(1)} %shard_map.76, bf16[512,4096]{1,0:T(8,128)(2,1)S(1)} %bitcast.13), kind=kOutput, calls=%fused_computation.1 | convolution fusion | flops 2155872256 | bytes 8912896 | tf_op jit(solution)/shard_map/dot_general | solution.py:36
  135.6 9.8 %all-to-all-start.1 = ((bf16[32,16,4096]{2,1,0:T(8,128)(2,1)}), bf16[32,16,4096]{2,1,0:T(8,128)(2,1)}, u32[]{:S(2)}, u32[]{:S(2)}) async-start(bf16[32,16,4096]{2,1,0:T(8,128)(2,1)} %bitcast.11), calls=%async_computation.1 | async-start | bytes 8388608 | tf_op jit(solution)/shard_map/all_to_all | solution.py:114
  145.4 0.1 copy.8
  145.5 148.0 %all-gather = f32[1024,1,16]{2,1,0:T(1,128)S(1)} all-gather(f32[32,1,16]{2,1,0:T(1,128)S(1)} %copy.8), channel_id=2, replica_groups=mesh['dp'=32,'tensor'=4] {'dp'}, dimensions={0}, use_global_device_ids=true | all-gather | bytes 67584 | tf_op jit(solution)/shard_map/all_gather | solution.py:106
  293.5 0.1 bitcast_reduce_fusion
  293.6 0.1 copy.11
  293.7 0.1 copy.10
  293.8 0.1 broadcast_in_dim.21
  293.9 0.3 copy.12
  294.3 0.0 all-to-all-done.1
  294.3 5.7 %multiply_convert_fusion = bf16[32,16,4096]{2,1,0:T(8,128)(2,1)} fusion(bf16[32,16,4096]{2,1,0:T(8,128)(2,1)} %all-to-all-done.1, bf16[32,16,4096]{2,1,0:T(8,128)(2,1)} %param.5, f32[32,4096]{1,0:T(8,128)S(1)} %broadcast_select_fusion), kind=kLoop, calls=%fused_computation | loop fusion | flops 14680064 | bytes 13107200 | tf_op jit(solution)/shard_map/convert_element_type | solution.py:92
  300.0 4.7 %copy.15 = bf16[32,16,4096]{2,1,0:T(8,128)(2,1)} copy(bf16[32,16,4096]{2,1,0:T(8,128)(2,1)} %all-to-all-done.1) | data formatting | bytes 8388608
  (10 shorter events, 0.1 us)
Async XLA Ops:
  7.2 111.2 %all-reduce.2.cloned.1.call-start = ((), (), s32[]{:S(2)}) async-start(), calls=%async_computation.2 | async-start | bytes 2097152 | tf_op jit(solution)/shard_map/psum | solution.py:83
  12.4 63.7 %copy-start.1 = (bf16[32,16,4096]{2,1,0:T(8,128)(2,1)}, bf16[32,16,4096]{2,1,0:T(8,128)(2,1)S(1)}, u32[]{:S(2)}) copy-start(bf16[32,16,4096]{2,1,0:T(8,128)(2,1)S(1)} %multiply_convert_fusion.2) | copy-start | bytes 12582916
  76.1 2.0 copy-start.2
  118.4 1.2 copy-start
  119.6 11.6 %copy-start.3 = (bf16[32,16,4096]{2,1,0:T(8,128)(2,1)S(1)}, bf16[32,16,4096]{2,1,0:T(8,128)(2,1)}, u32[]{:S(2)}) copy-start(bf16[32,16,4096]{2,1,0:T(8,128)(2,1)} %copy-done.2) | copy-start | bytes 12582916
  135.6 9.8 %copy-start.4 = (f32[32,1,16]{0,2,1:T(8,128)S(1)}, f32[32,1,16]{0,2,1:T(8,128)}, u32[]{:S(2)}) copy-start(f32[32,1,16]{0,2,1:T(8,128)} %param.9) | copy-start | bytes 6148
  135.6 158.7 %all-to-all-start.1 = ((bf16[32,16,4096]{2,1,0:T(8,128)(2,1)}), bf16[32,16,4096]{2,1,0:T(8,128)(2,1)}, u32[]{:S(2)}, u32[]{:S(2)}) async-start(bf16[32,16,4096]{2,1,0:T(8,128)(2,1)} %bitcast.11), calls=%async_computation.1 | async-start | bytes 8388608 | tf_op jit(solution)/shard_map/all_to_all | solution.py:114
Sparse Core Ops, SparseCore 0:
  81.6 36.7 all-reduce.1

commit v2 on v0

v2 whole, which is shorter than its diff:
```python
import functools
import math

import jax
import jax.numpy as jnp
from jax import lax
from jax.experimental import pallas as pl
from jax.experimental.pallas import tpu as pltpu
from jax.sharding import PartitionSpec as P

LATENT = 512
KEY_DIM = 128
VALUE_DIM = 128
ITERS = 5
KV_OUT = 16384


momentum_decay = 0.95
first_coef = 3.4445
second_coef = -4.775
third_coef = 2.0315
epsilon = 1e-07
clip_limit = 100.0
learn_rate = 0.02
weight_decay = 0.1

f32 = jnp.float32
bf16 = jnp.bfloat16
MIB = 2**20
TILE = 128
GR = 256
HALF = GR * 3 // 2
VMEM = pl.BlockSpec(memory_space=pltpu.VMEM)
SMEM = pl.BlockSpec(memory_space=pltpu.SMEM)
HBM = pl.BlockSpec(memory_space=pltpu.HBM)


def dot(left, right):
    return jnp.dot(left, right, preferred_element_type=f32)


def dot_nt(left, right):
    return lax.dot_general(left, right, (((1,), (1,)), ((), ())), preferred_element_type=f32)


def eye_tile():
    shape = (TILE, TILE)
    return lax.broadcasted_iota(jnp.int32, shape, 0) == lax.broadcasted_iota(jnp.int32, shape, 1)


def tiles_of(ref):
    return [pl.ds(i * TILE, TILE) for i in range(ref.shape[0] // TILE)]


def gram_kernel(core_ref, x_ref, keep_ref, give_ref):
    top = x_ref[0:GR, :]
    bottom = x_ref[GR:, :]
    parts = (dot_nt(top, top), dot_nt(top, bottom), dot_nt(bottom, bottom))
    for core, (low, high) in enumerate(((keep_ref, give_ref), (give_ref, keep_ref))):

        @pl.when(core_ref[0] == core)
        def _():
            low[0:GR, :] = parts[0]
            low[GR:, :] = parts[1][0 : GR // 2]
            high[0:GR, :] = parts[2]
            high[GR:, :] = parts[1][GR // 2 :]


def gram_halves(core, x):
    rows, cols = x.shape
    half = jax.ShapeDtypeStruct((HALF, GR), f32)
    return pl.pallas_call(
        gram_kernel,
        out_shape=(half, half),
        in_specs=[SMEM, VMEM],
        out_specs=(VMEM, VMEM),
        compiler_params=pltpu.CompilerParams(vmem_limit_bytes=32 * MIB),
        cost_estimate=pl.CostEstimate(
            flops=rows * rows * cols * 3 // 2, bytes_accessed=rows * cols * 2, transcendentals=0
        ),
    )(core, x)


def split_diagonal(full_ref, off_ref):
    eye = eye_tile()
    off_ref[...] = full_ref[...].astype(bf16)
    rows, cols = [], []
    for at in tiles_of(full_ref):
        tile = full_ref[at, at].astype(f32)
        on = jnp.where(eye, tile, 0.0)
        off_ref[at, at] = jnp.where(eye, 0.0, tile).astype(bf16)
        rows.append(jnp.sum(on, axis=0, keepdims=True))
        cols.append(jnp.sum(on, axis=1, keepdims=True))
    return jnp.concatenate(rows, 1), jnp.concatenate(cols, 0)


def less_diagonal(ref, col, row):
    eye = eye_tile()
    for i, at in enumerate(tiles_of(ref)):
        span = slice(i * TILE, (i + 1) * TILE)
        ref[at, at] = ref[at, at] - jnp.where(eye, col[span] * row[:, span], 0.0)


def newton_schulz(gram, half, total, poly, gram_off, half_off, total_off, poly_off):
    eye = eye_tile()
    trace = 0.0
    for at in tiles_of(gram):
        trace = trace + jnp.sum(jnp.where(eye, gram[at, at], 0.0))
    scale = 1.0 / (jnp.sqrt(trace) + epsilon)
    gram[...] = gram[...] * scale * scale
    for iteration in range(ITERS):
        g_row, g_col = split_diagonal(gram, gram_off)
        half[...] = third_coef * dot(gram_off[...], gram_off[...]) + gram[...] * (
            second_coef + third_coef * (g_col + g_row)
        )
        less_diagonal(half, third_coef * g_col, g_row)
        poly[...] = half[...].astype(bf16)
        p_row, p_col = split_diagonal(poly, poly_off)
        if iteration == 0:
            total[...] = poly[...].astype(f32)
            for at in tiles_of(total):
                total[at, at] = total[at, at] + jnp.where(eye, first_coef, 0.0)
        else:
            t_row, t_col = split_diagonal(total, total_off)
            total[...] = (
                dot(poly_off[...], total_off[...])
                + (first_coef + p_col) * total[...]
                + poly[...].astype(f32) * t_row
            )
            less_diagonal(total, p_col, t_row)
        if iteration < ITERS - 1:
            half[...] = (
                dot(poly_off[...], gram_off[...])
                + (first_coef + p_col) * gram[...]
                + poly[...].astype(f32) * g_row
            )
            less_diagonal(half, p_col, g_row)
            h_row, h_col = split_diagonal(half, half_off)
            gram[...] = (
                dot(half_off[...], poly_off[...])
                + half[...] * (first_coef + p_row)
                + h_col * poly[...].astype(f32)
            )
            less_diagonal(gram, h_col, p_row)
    return scale


def peak_block(peak):
    high = peak.astype(bf16).astype(f32)
    rest = peak - high
    middle = rest.astype(bf16).astype(f32)
    low = (rest - middle).astype(bf16).astype(f32)
    return (high + pltpu.roll(middle, 32, 1) + pltpu.roll(low, 64, 1)).astype(bf16)


def update_kernel(
    update_scale, width, rows_here,
    core_ref, mine_ref, other_ref, peak_ref, x_ref, weight_hbm, out_ref, weight_ref,
    gram, half, total, poly, gram_off, half_off, total_off, poly_off, factors, weight_sem,
):
    fetch = pltpu.make_async_copy(weight_hbm, weight_ref, weight_sem)
    fetch.start()
    for core, (low, high) in enumerate(((mine_ref, other_ref), (other_ref, mine_ref))):

        @pl.when(core_ref[0] == core)
        def _():
            gram[0:GR, 0:GR] = low[0:GR, :]
            gram[GR:, GR:] = high[0:GR, :]
            cross = jnp.concatenate([low[GR:, :], high[GR:, :]], 0)
            gram[0:GR, GR:] = cross
            gram[GR:, 0:GR] = cross.T

    scale = newton_schulz(
        gram, half, total, poly, gram_off, half_off, total_off, poly_off
    )
    factors[...] = (total[...] * scale).astype(bf16)
    rows, cols = x_ref.shape

    @pl.loop(0, cols // width)
    def _(step):
        at = pl.ds(pl.multiple_of(step * width, width), width)
        ortho = dot(factors[...], x_ref[:, at]).astype(bf16)
        out_ref[:, at] = (update_scale * ortho.astype(f32)).astype(bf16)

    block = peak_block(peak_ref[...])
    for i in range(rows // rows_here):
        out_ref[pl.ds(i * rows_here, rows_here), pl.ds(cols, TILE)] = block
    fetch.wait()


def scaled_update(core, mine, other, peak, x, kv_weight):
    rows, cols = x.shape
    square = (rows, rows)
    return pl.pallas_call(
        functools.partial(
            update_kernel, 0.2 * math.sqrt(max(LATENT, KV_OUT)), 1024, kv_weight.shape[1]
        ),
        out_shape=(
            jax.ShapeDtypeStruct((rows, cols + TILE), bf16),
            jax.ShapeDtypeStruct(kv_weight.shape, bf16),
        ),
        in_specs=[SMEM, VMEM, VMEM, VMEM, VMEM, HBM],
        out_specs=(VMEM, VMEM),
        scratch_shapes=[pltpu.VMEM(square, f32)] * 3
        + [pltpu.VMEM(square, bf16)] * 6
        + [pltpu.SemaphoreType.DMA],
        compiler_params=pltpu.CompilerParams(vmem_limit_bytes=45 * MIB),
        cost_estimate=pl.CostEstimate(
            flops=34 * rows**3 + 2 * rows * rows * cols,
            bytes_accessed=rows * cols * 4,
            transcendentals=0,
        ),
    )(core, mine, other, peak, x, kv_weight)


def gram_sum(core, x):
    other_core = [(i, i ^ 1) for i in range(4)]
    other_chip = [(i, i ^ 2) for i in range(4)]
    keep, give = gram_halves(core, x)
    mine = keep + lax.ppermute(give, "tensor", other_core)
    mine = mine + lax.ppermute(mine, "tensor", other_chip)
    return mine, lax.ppermute(mine, "tensor", other_core)


def step_kernel(weight_ref, recv_ref, update_hbm, new_ref, factor_ref, update_sem):
    step = pl.program_id(0)
    layers, rows, cols = weight_ref.shape
    group = new_ref.shape[0]
    store = pltpu.make_async_copy(recv_ref.at[:, :, pl.ds(0, cols)], update_hbm, update_sem)

    @pl.when(step == 0)
    def _():
        store.start()
        parts = recv_ref[:, :, pl.ds(cols, TILE)].astype(f32)
        peak = None
        for i in range(layers):
            high = parts[i]
            joined = high + pltpu.roll(high, TILE - 32, 1) + pltpu.roll(high, TILE - 64, 1)
            peak = joined if peak is None else jnp.maximum(peak, joined)
        factor_ref[...] = jnp.sqrt(jnp.minimum(1.0, clip_limit / peak))

    heads = cols // (2 * TILE)
    lane = lax.broadcasted_iota(jnp.int32, factor_ref.shape, 1)
    for i in range(group):
        layer = step * group + i
        factors = jnp.sum(jnp.where(lane == layer, factor_ref[...], 0.0), axis=1, keepdims=True)
        for head in range(heads):
            for part in range(2):
                at = pl.ds((2 * head + part) * TILE, TILE)
                stepped = weight_ref[layer, :, at].astype(f32) * (
                    1.0 - learn_rate * weight_decay
                ) - learn_rate * recv_ref[layer, :, at].astype(f32)
                if part == 0:
                    stepped = factors[head : head + 1, :] * stepped
                new_ref[i, :, at] = stepped.astype(bf16)

    @pl.when(step == pl.num_programs(0) - 1)
    def _():
        store.wait()


def apply_step(kv_weight, received):
    layers, rows, cols = kv_weight.shape
    group = layers // 4
    shape = jax.ShapeDtypeStruct(kv_weight.shape, bf16)
    return pl.pallas_call(
        step_kernel,
        grid=(layers // group,),
        out_shape=(shape, shape),
        in_specs=[VMEM, VMEM],
        out_specs=(
            pl.BlockSpec(memory_space=pl.ANY),
            pl.BlockSpec((group, rows, cols), lambda i: (i, 0, 0)),
        ),
        scratch_shapes=[pltpu.VMEM((rows, TILE), f32), pltpu.SemaphoreType.DMA],
        compiler_params=pltpu.CompilerParams(vmem_limit_bytes=24 * MIB),
        cost_estimate=pl.CostEstimate(
            flops=4 * layers * rows * cols, bytes_accessed=8 * layers * rows * cols, transcendentals=0
        ),
    )(kv_weight, received)


def on_device(kv_weight, momentum, gradient, head_counts, logit_peaks):
    layers, rows, shard_width = momentum.shape
    heads_here = shard_width // (KEY_DIM + VALUE_DIM)
    tensor_index = lax.axis_index("tensor")
    core = (tensor_index % 2).astype(jnp.int32).reshape(1)
    head_of = tensor_index * heads_here + jnp.arange(shard_width) // (KEY_DIM + VALUE_DIM)
    live_mask = (head_of[None, :] < head_counts[:, None]).astype(f32)
    new_momentum = (
        live_mask[:, None, :]
        * (momentum_decay * momentum.astype(f32) + gradient.astype(f32))
    ).astype(bf16)
    peaks = jnp.pad(logit_peaks[:, 0, :].T, ((0, 0), (0, TILE - layers)))
    new_momentum, peaks, core = lax.optimization_barrier((new_momentum, peaks, core))
    owned = lax.all_to_all(new_momentum, "dp", split_axis=0, concat_axis=0, tiled=True)
    owned = owned.reshape(layers * rows, shard_width)
    mine, other = gram_sum(core, owned)
    owned_update, weight = scaled_update(
        core, mine, other, peaks, owned, kv_weight
    )
    received = lax.all_to_all(
        owned_update.reshape(layers, rows, shard_width + TILE),
        "dp",
        split_axis=0,
        concat_axis=0,
        tiled=True,
    )
    update, new_weight = apply_step(weight, received)
    return (update, new_weight, new_momentum)


def solution(mesh):
    placed = (
        P(None, "dp", "tensor"),
        P(None, "dp", "tensor"),
        P(None, "dp", "tensor"),
        P(),
        P(None, "dp", "tensor"),
    )
    return jax.shard_map(
        on_device,
        mesh=mesh,
        in_specs=placed,
        out_specs=(P(None, "dp", "tensor"), P(None, "dp", "tensor"), P(None, "dp", "tensor")),
        check_vma=False,
    )
```

time: 622 us -> 164 us (0.26); the launches traced: 614 us -> 163 us
  waiting for transfers between devices: 206 us -> 13.9 us
  blocking collectives: 210 us -> 123 us
  local copies, waits for them, and re-layouts: 69.3 us -> 0.71 us
  matrix products: 65.8 us -> 0 us
  other arithmetic: 37.9 us -> 5.25 us
  Pallas kernels: 0 us -> 18.9 us
  between operations: 15 us -> 0.71 us
  starting transfers between devices: 10.5 us -> 0.88 us
    psum x5 -> x0, waiting for transfers between devices: 206 us -> none  [orthogonalize(): gram_matrix = lax.psum(local_gram, 'tensor')]
    pmax x1 -> x0, blocking collectives: 146 us -> none  [on_device(): head_peak = lax.pmax(logit_peaks, 'dp')]
    dot_general x15 -> x0, matrix products: 65.8 us -> none  [the longest x5 29.3 us: orthogonalize(): product = jnp.dot(polynomial, current, preferred_element_type=jnp.float32)]
    all_to_all x1 -> x2, blocking collectives: 63.7 us -> 123 us  [the longest x1 63.7 us: on_device(): lax.all_to_all(new_momentum, 'dp', split_axis=0, concat_axis=0, tiled=True)]
    unnamed x23 -> x2, local copies, waits for them, and re-layouts: 46.7 us -> 0.01 us
    unnamed x1 -> x0, other arithmetic: 27.5 us -> none
    broadcast_in_dim x2 -> x0, local copies, waits for them, and re-layouts: 22.4 us -> none  [the longest x1 22.3 us: on_device(): owned_update[None]]
    pallas_call x0 -> x3, Pallas kernels: none -> 18.9 us  [the longest x1 12.7 us: scaled_update(): pl.pallas_call(functools.partial(update_kernel, 0.2 * math.sqrt(max(LATEN...]
  transfers between devices with their start and end apart: 6 -> 3, of which waited for: 5 -> 3; matrix products, arithmetic and copies ran while one was open for 0% -> 0% of each run, Pallas kernels for 0% -> 0%
where the time goes in v2:
time: 164 us; the launch traced here: 163 us
  blocking collectives  123 us (75%)
  Pallas kernels  18.9 us (12%)
  waiting for transfers between devices  13.9 us (8%)
  other arithmetic  5.25 us (3%)
    all_to_all x1, blocking collectives, on_device(): lax.all_to_all(new_momentum, 'dp', split_axis=0, concat_axis=0, tiled=True)  63.7 us
    all_to_all x1, blocking collectives, on_device(): lax.all_to_all(owned_update.reshape(layers, rows, shard_width + TILE), 'd...  59.1 us
    pallas_call x1, Pallas kernels, scaled_update(): pl.pallas_call(functools.partial(update_kernel, 0.2 * math.sqrt(max(LATEN...  12.7 us
    ppermute x1, waiting for transfers between devices, gram_sum(): mine = mine + lax.ppermute(mine, 'tensor', other_chip)  10.5 us
    convert_element_type x1, other arithmetic, on_device(): new_momentum = (live_mask[:, None, :] * (momentum_decay * momentum.astype...  4.38 us
    pallas_call x1, Pallas kernels, apply_step(): pl.pallas_call(step_kernel, grid=(layers // group,), out_shape=(shape, sh...  4.35 us
  transfers between devices with their start and end apart: 3, of which 3 were waited for; matrix products, arithmetic and copies ran while one was open for 0% of the time, Pallas kernels for 0%

profile of v2, /device:TPU:0, one launch (start us, length us, event | category | flops | bytes accessed | tf_op | source)
XLA Modules:
  0.0 163.3 jit_solution(7058737756513872023)
XLA Ops:
  0.7 0.7 pad.4.peak_ref
  1.4 0.8 compare_convert_fusion
  2.1 4.4 %multiply_convert_fusion = bf16[32,16,4096]{2,1,0:T(8,128)(2,1)S(1)} fusion(bf16[32,16,4096]{2,1,0:T(8,128)(2,1)} %param.7, bf16[32,16,4096]{2,1,0:T(8,128)(2,1)} %param.6, f32[32,4096]{1,0:T(8,128)S(1)} %compare_convert_fusion), kind=kLoop, calls=%fused_computation | loop fusion | flops 12582912 | bytes 13107200 | tf_op jit(solution)/shard_map/convert_element_type | solution.py:293
  6.5 0.0 copy-start
  6.5 63.7 %all_to_all.10 = bf16[32,16,4096]{2,1,0:T(8,128)(2,1)S(1)} all-to-all(bf16[32,16,4096]{2,1,0:T(8,128)(2,1)S(1)} %multiply_convert_fusion), channel_id=1, replica_groups=mesh['dp'=32,'tensor'=4] {'dp'}, dimensions={0} | all-to-all | bytes 8388608 | tf_op jit(solution)/shard_map/all_to_all | solution.py:296
  70.2 0.0 copy-done
  70.3 1.9 %shard_map.76 = (f32[384,256]{1,0:T(8,128)S(1)}, f32[384,256]{1,0:T(8,128)S(1)}) custom-call(s32[1]{0:T(128)} %bitcast.2.core_ref, bf16[512,4096]{1,0:T(8,128)(2,1)S(1)} %bitcast.6), custom_call_target="tpu_custom_call" | custom-call | flops 1610612736 | bytes 4194304 | tf_op jit(solution)/shard_map/pallas_call | solution.py:72
  72.1 0.1 collective-permute-start
  72.2 1.7 %collective-permute-done = f32[384,256]{1,0:T(8,128)S(1)} collective-permute-done((f32[384,256]{1,0:T(8,128)S(1)}, f32[384,256]{1,0:T(8,128)S(1)}, u32[]{:S(2)}, u32[]{:S(2)}) %collective-permute-start) | collective-permute-done | bytes 393248 | tf_op jit(solution)/shard_map/ppermute | solution.py:220
  73.9 0.1 add.34
  74.0 0.7 collective-permute-start.1
  74.7 10.5 %collective-permute-done.1 = f32[384,256]{1,0:T(8,128)S(1)} collective-permute-done((f32[384,256]{1,0:T(8,128)S(1)}, f32[384,256]{1,0:T(8,128)S(1)}, u32[]{:S(2)}, u32[]{:S(2)}) %collective-permute-start.1) | collective-permute-done | bytes 393248 | tf_op jit(solution)/shard_map/ppermute | solution.py:221
  85.2 0.1 add.35.mine_ref
  85.3 0.1 collective-permute-start.2
  85.4 1.7 %collective-permute-done.2.other_ref = f32[384,256]{1,0:T(8,128)S(1)} collective-permute-done((f32[384,256]{1,0:T(8,128)S(1)}, f32[384,256]{1,0:T(8,128)S(1)}, u32[]{:S(2)}, u32[]{:S(2)}) %collective-permute-start.2) | collective-permute-done | bytes 393248 | tf_op jit(solution)/shard_map/ppermute | solution.py:222
  87.1 12.7 %shard_map.77 = (bf16[512,4224]{1,0:T(8,128)(2,1)}, bf16[32,16,4096]{2,1,0:T(8,128)(2,1)S(1)}) custom-call(s32[1]{0:T(128)} %bitcast.2.core_ref, f32[384,256]{1,0:T(8,128)S(1)} %add.35.mine_ref, f32[384,256]{1,0:T(8,128)S(1)} %collective-permute-done.2.other_ref, f32[16,128]{1,0:T(8,128)S(1)} %pad.4.peak_ref, bf16[512,4096]{1,0:T(8,128)(2,1)S(1)} %bitcast.7, ...), custom_call_target="tpu_custom_call" | custom-call | flops 6710886400 | bytes 8388608 | tf_op jit(solution)/shard_map/pallas_call | solution.py:194
  99.8 59.1 %all_to_all.11.recv_ref = bf16[32,16,4224]{2,1,0:T(8,128)(2,1)S(1)} all-to-all(bf16[32,16,4224]{2,1,0:T(8,128)(2,1)} %bitcast.8), channel_id=1, replica_groups=mesh['dp'=32,'tensor'=4] {'dp'}, dimensions={0} | all-to-all | bytes 8650752 | tf_op jit(solution)/shard_map/all_to_all | solution.py:302
  158.9 4.4 %shard_map.78 = (bf16[32,16,4096]{2,1,0:T(8,128)(2,1)}, bf16[32,16,4096]{2,1,0:T(8,128)(2,1)}) custom-call(bf16[32,16,4096]{2,1,0:T(8,128)(2,1)S(1)} %get-tuple-element.17.weight_ref, bf16[32,16,4224]{2,1,0:T(8,128)(2,1)S(1)} %all_to_all.11.recv_ref), custom_call_target="tpu_custom_call" | custom-call | flops 8388608 | bytes 16777216 | tf_op jit(solution)/shard_map/pallas_call | solution.py:266
  (1 shorter events, 0.0 us)
Async XLA Ops:
  6.5 63.7 %copy-start = (bf16[32,16,4096]{2,1,0:T(8,128)(2,1)}, bf16[32,16,4096]{2,1,0:T(8,128)(2,1)S(1)}, u32[]{:S(2)}) copy-start(bf16[32,16,4096]{2,1,0:T(8,128)(2,1)S(1)} %multiply_convert_fusion) | copy-start | bytes 12582916
  72.1 1.8 %collective-permute-start = (f32[384,256]{1,0:T(8,128)S(1)}, f32[384,256]{1,0:T(8,128)S(1)}, u32[]{:S(2)}, u32[]{:S(2)}) collective-permute-start(f32[384,256]{1,0:T(8,128)S(1)} %get-tuple-element.15), channel_id=1, source_target_pairs={{0,1},{1,0},{2,3},{3,2},{4,5},{5,4},{6,7},{7,6},{8,9},{9,8},{10,11... | collective-permute-start | bytes 1179656 | tf_op jit(solution)/shard_map/ppermute | solution.py:220
  74.0 11.2 %collective-permute-start.1 = (f32[384,256]{1,0:T(8,128)S(1)}, f32[384,256]{1,0:T(8,128)S(1)}, u32[]{:S(2)}, u32[]{:S(2)}) collective-permute-start(f32[384,256]{1,0:T(8,128)S(1)} %add.34), channel_id=1, source_target_pairs={{0,2},{1,3},{2,0},{3,1},{4,6},{5,7},{6,4},{7,5},{8,10},{9,11},{10,... | collective-permute-start | bytes 1179656 | tf_op jit(solution)/shard_map/ppermute | solution.py:221
  85.3 1.8 %collective-permute-start.2 = (f32[384,256]{1,0:T(8,128)S(1)}, f32[384,256]{1,0:T(8,128)S(1)}, u32[]{:S(2)}, u32[]{:S(2)}) collective-permute-start(f32[384,256]{1,0:T(8,128)S(1)} %add.35.mine_ref), channel_id=1, source_target_pairs={{0,1},{1,0},{2,3},{3,2},{4,5},{5,4},{6,7},{7,6},{8,9},{9,8},{10,11... | collective-permute-start | bytes 1179656 | tf_op jit(solution)/shard_map/ppermute | solution.py:222

commit v3 on v2

--- a/solution.py
+++ b/solution.py
@@ -29,7 +29,7 @@
 MIB = 2**20
 TILE = 128
 GR = 256
-HALF = GR * 3 // 2
+HALF = 4 * TILE + 8
 VMEM = pl.BlockSpec(memory_space=pltpu.VMEM)
 SMEM = pl.BlockSpec(memory_space=pltpu.SMEM)
 HBM = pl.BlockSpec(memory_space=pltpu.HBM)
@@ -52,53 +52,84 @@
     return [pl.ds(i * TILE, TILE) for i in range(ref.shape[0] // TILE)]
 
 
-def gram_kernel(core_ref, x_ref, keep_ref, give_ref):
-    top = x_ref[0:GR, :]
-    bottom = x_ref[GR:, :]
-    parts = (dot_nt(top, top), dot_nt(top, bottom), dot_nt(bottom, bottom))
-    for core, (low, high) in enumerate(((keep_ref, give_ref), (give_ref, keep_ref))):
-
-        @pl.when(core_ref[0] == core)
+def pack_half(half_ref, square, across):
+    row = lax.broadcasted_iota(jnp.int32, (TILE, TILE), 0)
+    col = lax.broadcasted_iota(jnp.int32, (TILE, TILE), 1)
+    first, second = square[:TILE, :TILE], square[TILE:, TILE:]
+    half_ref[pl.ds(0, TILE), :] = jnp.where(row <= col, first, second)
+    half_ref[pl.ds(TILE, TILE), :] = square[:TILE, TILE:]
+    half_ref[pl.ds(2 * TILE, TILE), :] = across[:, :TILE]
+    half_ref[pl.ds(3 * TILE, TILE), :] = across[:, TILE:]
+    diagonal = jnp.sum(jnp.where(row == col, second, 0.0), axis=0, keepdims=True)
+    half_ref[pl.ds(4 * TILE, 8), :] = jnp.broadcast_to(diagonal, (8, TILE))
+
+
+def unpack_half(half_ref, gram, which):
+    row = lax.broadcasted_iota(jnp.int32, (TILE, TILE), 0)
+    col = lax.broadcasted_iota(jnp.int32, (TILE, TILE), 1)
+
+    def put(i, j, tile):
+        gram[pl.ds(i * TILE, TILE), pl.ds(j * TILE, TILE)] = tile
+
+    both = half_ref[pl.ds(0, TILE), :]
+    turned = both.T
+    base = 2 * which
+    put(base, base, jnp.where(row <= col, both, turned))
+    second = jnp.where(row > col, both, turned)
+    put(base + 1, base + 1, jnp.where(row == col, half_ref[pl.ds(4 * TILE, 1), :], second))
+    for k, (i, j) in enumerate(((base, base + 1), (which, 2), (which, 3))):
+        tile = half_ref[pl.ds((k + 1) * TILE, TILE), :]
+        put(i, j, tile)
+        put(j, i, tile.T)
+
+
+def gram_kernel(own, core_ref, x_ref, half_ref):
+    for which in range(2):
+
+        @pl.when(core_ref[0] == (which if own else 1 - which))
         def _():
-            low[0:GR, :] = parts[0]
-            low[GR:, :] = parts[1][0 : GR // 2]
-            high[0:GR, :] = parts[2]
-            high[GR:, :] = parts[1][GR // 2 :]
-
-
-def gram_halves(core, x):
+            block = x_ref[pl.ds(which * GR, GR), :]
+            band = x_ref[pl.ds(which * TILE, TILE), :]
+            pack_half(half_ref, dot_nt(block, block), dot_nt(band, x_ref[pl.ds(GR, GR), :]))
+
+
+def gram_half(own, core, x):
     rows, cols = x.shape
-    half = jax.ShapeDtypeStruct((HALF, GR), f32)
     return pl.pallas_call(
-        gram_kernel,
-        out_shape=(half, half),
+        functools.partial(gram_kernel, own),
+        out_shape=jax.ShapeDtypeStruct((HALF, TILE), f32),
         in_specs=[SMEM, VMEM],
-        out_specs=(VMEM, VMEM),
+        out_specs=VMEM,
         compiler_params=pltpu.CompilerParams(vmem_limit_bytes=32 * MIB),
         cost_estimate=pl.CostEstimate(
-            flops=rows * rows * cols * 3 // 2, bytes_accessed=rows * cols * 2, transcendentals=0
+            flops=rows * rows * cols * 3 // 4, bytes_accessed=rows * cols * 2, transcendentals=0
         ),
     )(core, x)
 
 
-def split_diagonal(full_ref, off_ref):
+def to_col(row):
+    tiles = [row[:, i : i + TILE] for i in range(0, row.shape[1], TILE)]
+    return jnp.concatenate([jnp.broadcast_to(t, (8, TILE)).T[:, 0:1] for t in tiles], 0)
+
+
+def settle(value, extra, full_ref, off_ref):
     eye = eye_tile()
-    off_ref[...] = full_ref[...].astype(bf16)
-    rows, cols = [], []
-    for at in tiles_of(full_ref):
-        tile = full_ref[at, at].astype(f32)
-        on = jnp.where(eye, tile, 0.0)
+    kind = full_ref.dtype
+    full_ref[...] = value.astype(kind)
+    off_ref[...] = value.astype(bf16)
+    found = []
+    for i in range(0, value.shape[0], TILE):
+        at = pl.ds(i, TILE)
+        tile = value[i : i + TILE, i : i + TILE]
+        row = jnp.sum(jnp.where(eye, tile, 0.0), axis=0, keepdims=True)
+        if extra is not None:
+            row = row - extra[:, i : i + TILE]
+        if kind != f32:
+            row = row.astype(kind).astype(f32)
+        full_ref[at, at] = jnp.where(eye, row, tile).astype(kind)
         off_ref[at, at] = jnp.where(eye, 0.0, tile).astype(bf16)
-        rows.append(jnp.sum(on, axis=0, keepdims=True))
-        cols.append(jnp.sum(on, axis=1, keepdims=True))
-    return jnp.concatenate(rows, 1), jnp.concatenate(cols, 0)
-
-
-def less_diagonal(ref, col, row):
-    eye = eye_tile()
-    for i, at in enumerate(tiles_of(ref)):
-        span = slice(i * TILE, (i + 1) * TILE)
-        ref[at, at] = ref[at, at] - jnp.where(eye, col[span] * row[:, span], 0.0)
+        found.append(row)
+    return jnp.concatenate(found, 1)
 
 
 def newton_schulz(gram, half, total, poly, gram_off, half_off, total_off, poly_off):
@@ -107,41 +138,46 @@
     for at in tiles_of(gram):
         trace = trace + jnp.sum(jnp.where(eye, gram[at, at], 0.0))
     scale = 1.0 / (jnp.sqrt(trace) + epsilon)
-    gram[...] = gram[...] * scale * scale
+    g_row = settle(gram[...] * scale * scale, None, gram, gram_off)
     for iteration in range(ITERS):
-        g_row, g_col = split_diagonal(gram, gram_off)
-        half[...] = third_coef * dot(gram_off[...], gram_off[...]) + gram[...] * (
-            second_coef + third_coef * (g_col + g_row)
+        g_col = to_col(g_row)
+        square = third_coef * dot(gram_off[...], gram_off[...])
+        p_row = settle(
+            square + gram[...] * (second_coef + third_coef * (g_col + g_row)),
+            third_coef * g_row * g_row,
+            poly,
+            poly_off,
         )
-        less_diagonal(half, third_coef * g_col, g_row)
-        poly[...] = half[...].astype(bf16)
-        p_row, p_col = split_diagonal(poly, poly_off)
+        p_col = to_col(p_row)
+        if iteration < ITERS - 1:
+            h_row = settle(
+                dot(poly_off[...], gram_off[...])
+                + (first_coef + p_col) * gram[...]
+                + poly[...].astype(f32) * g_row,
+                p_row * g_row,
+                half,
+                half_off,
+            )
         if iteration == 0:
-            total[...] = poly[...].astype(f32)
-            for at in tiles_of(total):
-                total[at, at] = total[at, at] + jnp.where(eye, first_coef, 0.0)
+            t_row = settle(poly[...].astype(f32), jnp.full_like(p_row, -first_coef), total, total_off)
         else:
-            t_row, t_col = split_diagonal(total, total_off)
-            total[...] = (
+            t_row = settle(
                 dot(poly_off[...], total_off[...])
                 + (first_coef + p_col) * total[...]
-                + poly[...].astype(f32) * t_row
+                + poly[...].astype(f32) * t_row,
+                p_row * t_row,
+                total,
+                total_off,
             )
-            less_diagonal(total, p_col, t_row)
         if iteration < ITERS - 1:
-            half[...] = (
-                dot(poly_off[...], gram_off[...])
-                + (first_coef + p_col) * gram[...]
-                + poly[...].astype(f32) * g_row
-            )
-            less_diagonal(half, p_col, g_row)
-            h_row, h_col = split_diagonal(half, half_off)
-            gram[...] = (
+            g_row = settle(
                 dot(half_off[...], poly_off[...])
                 + half[...] * (first_coef + p_row)
-                + h_col * poly[...].astype(f32)
+                + to_col(h_row) * poly[...].astype(f32),
+                h_row * p_row,
+                gram,
+                gram_off,
             )
-            less_diagonal(gram, h_col, p_row)
     return scale
 
 
@@ -160,15 +196,12 @@
 ):
     fetch = pltpu.make_async_copy(weight_hbm, weight_ref, weight_sem)
     fetch.start()
-    for core, (low, high) in enumerate(((mine_ref, other_ref), (other_ref, mine_ref))):
+    for core, halves in enumerate(((mine_ref, other_ref), (other_ref, mine_ref))):
 
         @pl.when(core_ref[0] == core)
         def _():
-            gram[0:GR, 0:GR] = low[0:GR, :]
-            gram[GR:, GR:] = high[0:GR, :]
-            cross = jnp.concatenate([low[GR:, :], high[GR:, :]], 0)
-            gram[0:GR, GR:] = cross
-            gram[GR:, 0:GR] = cross.T
+            for which, half_ref in enumerate(halves):
+                unpack_half(half_ref, gram, which)
 
     scale = newton_schulz(
         gram, half, total, poly, gram_off, half_off, total_off, poly_off
@@ -176,9 +209,8 @@
     factors[...] = (total[...] * scale).astype(bf16)
     rows, cols = x_ref.shape
 
-    @pl.loop(0, cols // width)
-    def _(step):
-        at = pl.ds(pl.multiple_of(step * width, width), width)
+    for start in range(0, cols, width):
+        at = pl.ds(start, width)
         ortho = dot(factors[...], x_ref[:, at]).astype(bf16)
         out_ref[:, at] = (update_scale * ortho.astype(f32)).astype(bf16)
 
@@ -213,13 +245,16 @@
     )(core, mine, other, peak, x, kv_weight)
 
 
-def gram_sum(core, x):
+def gram_sum(core, x, peaks):
     other_core = [(i, i ^ 1) for i in range(4)]
     other_chip = [(i, i ^ 2) for i in range(4)]
-    keep, give = gram_halves(core, x)
-    mine = keep + lax.ppermute(give, "tensor", other_core)
+    given = lax.ppermute(gram_half(False, core, x), "tensor", other_core)
+    mine = gram_half(True, core, x) + given
+    mine, peaks = lax.optimization_barrier((mine, peaks))
+    peaks = jnp.pad(peaks, ((0, 0), (0, TILE - peaks.shape[1])))
     mine = mine + lax.ppermute(mine, "tensor", other_chip)
-    return mine, lax.ppermute(mine, "tensor", other_core)
+    mine, peaks = lax.optimization_barrier((mine, peaks))
+    return mine, lax.ppermute(mine, "tensor", other_core), peaks
 
 
 def step_kernel(weight_ref, recv_ref, update_hbm, new_ref, factor_ref, update_sem):
@@ -285,17 +320,18 @@
     heads_here = shard_width // (KEY_DIM + VALUE_DIM)
     tensor_index = lax.axis_index("tensor")
     core = (tensor_index % 2).astype(jnp.int32).reshape(1)
-    head_of = tensor_index * heads_here + jnp.arange(shard_width) // (KEY_DIM + VALUE_DIM)
-    live_mask = (head_of[None, :] < head_counts[:, None]).astype(f32)
+    head_of = tensor_index * heads_here + lax.broadcasted_iota(
+        jnp.int32, momentum.shape, 2
+    ) // (KEY_DIM + VALUE_DIM)
+    live_mask = (head_of < head_counts[:, None, None]).astype(f32)
     new_momentum = (
-        live_mask[:, None, :]
+        live_mask
         * (momentum_decay * momentum.astype(f32) + gradient.astype(f32))
     ).astype(bf16)
-    peaks = jnp.pad(logit_peaks[:, 0, :].T, ((0, 0), (0, TILE - layers)))
-    new_momentum, peaks, core = lax.optimization_barrier((new_momentum, peaks, core))
+    new_momentum, core = lax.optimization_barrier((new_momentum, core))
     owned = lax.all_to_all(new_momentum, "dp", split_axis=0, concat_axis=0, tiled=True)
     owned = owned.reshape(layers * rows, shard_width)
-    mine, other = gram_sum(core, owned)
+    mine, other, peaks = gram_sum(core, owned, logit_peaks[:, 0, :].T)
     owned_update, weight = scaled_update(
         core, mine, other, peaks, owned, kv_weight
     )

time: 164 us -> 158 us (0.963)
  waiting for transfers between devices: 13.9 us -> 9.66 us
    ppermute x1, waiting for transfers between devices: 10.5 us -> 7.95 us  [gram_sum(): mine = mine + lax.ppermute(mine, 'tensor', other_chip)]
    ppermute x2, waiting for transfers between devices: 3.42 us -> 1.71 us  [the longest x1 1.53 us: gram_sum(): return (mine, lax.ppermute(mine, 'tensor', other_core), peaks)]
    convert_element_type x2 -> x1, other arithmetic: 5.14 us -> 4.43 us  [on_device(): new_momentum = (live_mask * (momentum_decay * momentum.astype(f32) + grad...]
  transfers between devices with their start and end apart: 3 -> 3, of which waited for: 3 -> 3; matrix products, arithmetic and copies ran while one was open for 0% -> 0% of each run, Pallas kernels for 0% -> 1%
where the time goes in v3:
time: 158 us
  blocking collectives  123 us (78%)
  Pallas kernels  19.1 us (12%)
  waiting for transfers between devices  9.66 us (6%)
  other arithmetic  4.53 us (3%)
    all_to_all x1, blocking collectives, on_device(): lax.all_to_all(new_momentum, 'dp', split_axis=0, concat_axis=0, tiled=True)  63.7 us
    all_to_all x1, blocking collectives, on_device(): lax.all_to_all(owned_update.reshape(layers, rows, shard_width + TILE), 'd...  59.1 us
    pallas_call x1, Pallas kernels, scaled_update(): pl.pallas_call(functools.partial(update_kernel, 0.2 * math.sqrt(max(LATEN...  12.1 us
    ppermute x1, waiting for transfers between devices, gram_sum(): mine = mine + lax.ppermute(mine, 'tensor', other_chip)  7.95 us
    convert_element_type x1, other arithmetic, on_device(): new_momentum = (live_mask * (momentum_decay * momentum.astype(f32) + grad...  4.43 us
    pallas_call x1, Pallas kernels, apply_step(): pl.pallas_call(step_kernel, grid=(layers // group,), out_shape=(shape, sh...  4.29 us
  transfers between devices with their start and end apart: 3, of which 3 were waited for; matrix products, arithmetic and copies ran while one was open for 0% of the time, Pallas kernels for 1%

profile of v3, /device:TPU:0, one launch (start us, length us, event | category | flops | bytes accessed | tf_op | source)
XLA Modules:
  0.0 157.9 jit_solution(10071188903329862374)
XLA Ops:
  0.7 4.4 %select_convert_fusion = bf16[32,16,4096]{2,1,0:T(8,128)(2,1)S(1)} fusion(bf16[32,16,4096]{2,1,0:T(8,128)(2,1)} %param.7, bf16[32,16,4096]{2,1,0:T(8,128)(2,1)} %param.6, s32[32]{0:T(128)} %param.8, s32[4096]{0:T(1024)S(1)} %get-tuple-element.23, s32[4096]{0:T(1024)S(1)} %get-tuple-element.24, s32[]{:T(128)S(6)} %mul.12, pred[4096]{0:T(1024)(128)(4,1)S(1)} %fusion.2), kind=kLoop, calls=%fused_computation | loop fusion | flops 18874368 | bytes 12619908 | tf_op jit(solution)/shard_map/convert_element_type | solution.py:330
  5.1 0.0 copy-start
  5.1 63.7 %all_to_all.10 = bf16[32,16,4096]{2,1,0:T(8,128)(2,1)S(1)} all-to-all(bf16[32,16,4096]{2,1,0:T(8,128)(2,1)S(1)} %select_convert_fusion), channel_id=1, replica_groups=mesh['dp'=32,'tensor'=4] {'dp'}, dimensions={0} | all-to-all | bytes 8388608 | tf_op jit(solution)/shard_map/all_to_all | solution.py:332
  68.9 0.0 copy-start.1
  68.9 1.3 shard_map.77
  70.2 0.0 copy-done
  70.2 0.1 collective-permute-start
  70.3 1.3 shard_map.76
  71.6 0.2 collective-permute-done
  71.8 0.7 collective-permute-start.1
  72.6 0.0 copy-done.1
  72.6 7.9 %collective-permute-done.1 = f32[520,128]{1,0:T(8,128)S(1)} collective-permute-done((f32[520,128]{1,0:T(8,128)S(1)}, f32[520,128]{1,0:T(8,128)S(1)}, u32[]{:S(2)}, u32[]{:S(2)}) %collective-permute-start.1) | collective-permute-done | bytes 266272 | tf_op jit(solution)/shard_map/ppermute | solution.py:255
  80.6 0.1 collective-permute-start.2
  80.7 1.5 collective-permute-done.2.other_ref
  82.2 12.1 %shard_map.78 = (bf16[512,4224]{1,0:T(8,128)(2,1)}, bf16[32,16,4096]{2,1,0:T(8,128)(2,1)S(1)}) custom-call(s32[1]{0:T(128)} %bitcast.core_ref, f32[520,128]{1,0:T(8,128)S(1)} %add.28.mine_ref, f32[520,128]{1,0:T(8,128)S(1)} %collective-permute-done.2.other_ref, f32[16,128]{1,0:T(8,128)S(1)} %pad.4.peak_ref, bf16[512,4096]{1,0:T(8,128)(2,1)S(1)} %bitcast.8, ...), custom_call_target="tpu_custom_call" | custom-call | flops 6710886400 | bytes 8388608 | tf_op jit(solution)/shard_map/pallas_call | solution.py:226
  94.3 59.1 %all_to_all.11.recv_ref = bf16[32,16,4224]{2,1,0:T(8,128)(2,1)S(1)} all-to-all(bf16[32,16,4224]{2,1,0:T(8,128)(2,1)} %bitcast.9), channel_id=1, replica_groups=mesh['dp'=32,'tensor'=4] {'dp'}, dimensions={0} | all-to-all | bytes 8650752 | tf_op jit(solution)/shard_map/all_to_all | solution.py:338
  153.4 4.3 %shard_map.79 = (bf16[32,16,4096]{2,1,0:T(8,128)(2,1)}, bf16[32,16,4096]{2,1,0:T(8,128)(2,1)}) custom-call(bf16[32,16,4096]{2,1,0:T(8,128)(2,1)S(1)} %get-tuple-element.19.weight_ref, bf16[32,16,4224]{2,1,0:T(8,128)(2,1)S(1)} %all_to_all.11.recv_ref), custom_call_target="tpu_custom_call" | custom-call | flops 8388608 | bytes 16777216 | tf_op jit(solution)/shard_map/pallas_call | solution.py:301
  (5 shorter events, 0.1 us)
Async XLA Ops:
  5.1 65.1 %copy-start = (bf16[32,16,4096]{2,1,0:T(8,128)(2,1)}, bf16[32,16,4096]{2,1,0:T(8,128)(2,1)S(1)}, u32[]{:S(2)}) copy-start(bf16[32,16,4096]{2,1,0:T(8,128)(2,1)S(1)} %select_convert_fusion) | copy-start | bytes 12582916
  68.9 3.7 %copy-start.1 = (f32[32,1,16]{0,2,1:T(8,128)S(1)}, f32[32,1,16]{0,2,1:T(8,128)}, u32[]{:S(2)}) copy-start(f32[32,1,16]{0,2,1:T(8,128)} %param.9) | copy-start | bytes 6148
  70.2 1.6 %collective-permute-start = (f32[520,128]{1,0:T(8,128)S(1)}, f32[520,128]{1,0:T(8,128)S(1)}, u32[]{:S(2)}, u32[]{:S(2)}) collective-permute-start(f32[520,128]{1,0:T(8,128)S(1)} %shard_map.77), channel_id=1, source_target_pairs={{0,1},{1,0},{2,3},{3,2},{4,5},{5,4},{6,7},{7,6},{8,9},{9,8},{10,11... | collective-permute-start | bytes 798728 | tf_op jit(solution)/shard_map/ppermute | solution.py:251
  71.8 8.7 %collective-permute-start.1 = (f32[520,128]{1,0:T(8,128)S(1)}, f32[520,128]{1,0:T(8,128)S(1)}, u32[]{:S(2)}, u32[]{:S(2)}) collective-permute-start(f32[520,128]{1,0:T(8,128)S(1)} %add.27), channel_id=1, source_target_pairs={{0,2},{1,3},{2,0},{3,1},{4,6},{5,7},{6,4},{7,5},{8,10},{9,11},{10,... | collective-permute-start | bytes 798728 | tf_op jit(solution)/shard_map/ppermute | solution.py:255
  80.6 1.6 %collective-permute-start.2 = (f32[520,128]{1,0:T(8,128)S(1)}, f32[520,128]{1,0:T(8,128)S(1)}, u32[]{:S(2)}, u32[]{:S(2)}) collective-permute-start(f32[520,128]{1,0:T(8,128)S(1)} %add.28.mine_ref), channel_id=1, source_target_pairs={{0,1},{1,0},{2,3},{3,2},{4,5},{5,4},{6,7},{7,6},{8,9},{9,8},{10,11... | collective-permute-start | bytes 798728 | tf_op jit(solution)/shard_map/ppermute | solution.py:257

commit v4 on v3

--- a/solution.py
+++ b/solution.py
@@ -236,7 +236,7 @@
         scratch_shapes=[pltpu.VMEM(square, f32)] * 3
         + [pltpu.VMEM(square, bf16)] * 6
         + [pltpu.SemaphoreType.DMA],
-        compiler_params=pltpu.CompilerParams(vmem_limit_bytes=45 * MIB),
+        compiler_params=pltpu.CompilerParams(vmem_limit_bytes=36 * MIB),
         cost_estimate=pl.CostEstimate(
             flops=34 * rows**3 + 2 * rows * rows * cols,
             bytes_accessed=rows * cols * 4,

time: 158 us -> 156 us (0.987)
  Pallas kernels: 19.1 us -> 17.4 us
    pallas_call x1, Pallas kernels: 12.1 us -> 10.4 us  [scaled_update(): pl.pallas_call(functools.partial(update_kernel, 0.2 * math.sqrt(max(LATEN...]
where the time goes in v4:
time: 156 us; the launch traced here: 155 us
  blocking collectives  122 us (78%)
  Pallas kernels  17.4 us (11%)
  waiting for transfers between devices  9.66 us (6%)
  other arithmetic  4.53 us (3%)
    all_to_all x1, blocking collectives, on_device(): lax.all_to_all(new_momentum, 'dp', split_axis=0, concat_axis=0, tiled=True)  63.7 us
    all_to_all x1, blocking collectives, on_device(): lax.all_to_all(owned_update.reshape(layers, rows, shard_width + TILE), 'd...  58.3 us
    pallas_call x1, Pallas kernels, scaled_update(): pl.pallas_call(functools.partial(update_kernel, 0.2 * math.sqrt(max(LATEN...  10.4 us
    ppermute x1, waiting for transfers between devices, gram_sum(): mine = mine + lax.ppermute(mine, 'tensor', other_chip)  7.95 us
    convert_element_type x1, other arithmetic, on_device(): new_momentum = (live_mask * (momentum_decay * momentum.astype(f32) + grad...  4.43 us
    pallas_call x1, Pallas kernels, apply_step(): pl.pallas_call(step_kernel, grid=(layers // group,), out_shape=(shape, sh...  4.29 us
  transfers between devices with their start and end apart: 3, of which 3 were waited for; matrix products, arithmetic and copies ran while one was open for 0% of the time, Pallas kernels for 1%

profile of v4, /device:TPU:0, one launch (start us, length us, event | category | flops | bytes accessed | tf_op | source)
XLA Modules:
  0.0 155.3 jit_solution(1611665904291045922)
XLA Ops:
  0.7 4.4 %select_convert_fusion = bf16[32,16,4096]{2,1,0:T(8,128)(2,1)S(1)} fusion(bf16[32,16,4096]{2,1,0:T(8,128)(2,1)} %param.7, bf16[32,16,4096]{2,1,0:T(8,128)(2,1)} %param.6, s32[32]{0:T(128)} %param.8, s32[4096]{0:T(1024)S(1)} %get-tuple-element.23, s32[4096]{0:T(1024)S(1)} %get-tuple-element.24, s32[]{:T(128)S(6)} %mul.12, pred[4096]{0:T(1024)(128)(4,1)S(1)} %fusion.2), kind=kLoop, calls=%fused_computation | loop fusion | flops 18874368 | bytes 12619908 | tf_op jit(solution)/shard_map/convert_element_type | solution.py:330
  5.1 0.0 copy-start.1
  5.1 63.7 %all_to_all.10 = bf16[32,16,4096]{2,1,0:T(8,128)(2,1)S(1)} all-to-all(bf16[32,16,4096]{2,1,0:T(8,128)(2,1)S(1)} %select_convert_fusion), channel_id=1, replica_groups=mesh['dp'=32,'tensor'=4] {'dp'}, dimensions={0} | all-to-all | bytes 8388608 | tf_op jit(solution)/shard_map/all_to_all | solution.py:332
  68.9 0.0 copy-start.2
  68.9 0.0 copy-start
  68.9 1.3 shard_map.77
  70.2 0.0 copy-done.1
  70.2 0.1 collective-permute-start
  70.3 1.3 shard_map.76
  71.6 0.2 collective-permute-done
  71.8 0.7 collective-permute-start.1
  72.6 0.0 copy-done.2
  72.6 7.9 %collective-permute-done.1 = f32[520,128]{1,0:T(8,128)S(1)} collective-permute-done((f32[520,128]{1,0:T(8,128)S(1)}, f32[520,128]{1,0:T(8,128)S(1)}, u32[]{:S(2)}, u32[]{:S(2)}) %collective-permute-start.1) | collective-permute-done | bytes 266272 | tf_op jit(solution)/shard_map/ppermute | solution.py:255
  80.6 0.1 collective-permute-start.2
  80.7 1.5 collective-permute-done.2.other_ref
  82.2 0.0 copy-done
  82.2 10.4 %shard_map.78 = (bf16[512,4224]{1,0:T(8,128)(2,1)S(1)}, bf16[32,16,4096]{2,1,0:T(8,128)(2,1)S(1)}) custom-call(s32[1]{0:T(128)} %bitcast.core_ref, f32[520,128]{1,0:T(8,128)S(1)} %add.28.mine_ref, f32[520,128]{1,0:T(8,128)S(1)} %collective-permute-done.2.other_ref, f32[16,128]{1,0:T(8,128)S(1)} %pad.4.peak_ref, bf16[512,4096]{1,0:T(8,128)(2,1)S(1)} %bitcast.8, ...), custom_call_target="tpu_custom_call" | custom-call | flops 6710886400 | bytes 8388608 | tf_op jit(solution)/shard_map/pallas_call | solution.py:226
  92.6 58.3 %all_to_all.11.recv_ref = bf16[32,16,4224]{2,1,0:T(8,128)(2,1)S(1)} all-to-all(bf16[32,16,4224]{2,1,0:T(8,128)(2,1)S(1)} %bitcast.9), channel_id=1, replica_groups=mesh['dp'=32,'tensor'=4] {'dp'}, dimensions={0} | all-to-all | bytes 8650752 | tf_op jit(solution)/shard_map/all_to_all | solution.py:338
  150.9 4.3 %shard_map.79 = (bf16[32,16,4096]{2,1,0:T(8,128)(2,1)}, bf16[32,16,4096]{2,1,0:T(8,128)(2,1)}) custom-call(bf16[32,16,4096]{2,1,0:T(8,128)(2,1)S(1)} %get-tuple-element.19.weight_ref, bf16[32,16,4224]{2,1,0:T(8,128)(2,1)S(1)} %all_to_all.11.recv_ref), custom_call_target="tpu_custom_call" | custom-call | flops 8388608 | bytes 16777216 | tf_op jit(solution)/shard_map/pallas_call | solution.py:301
  (5 shorter events, 0.1 us)
Async XLA Ops:
  5.1 65.1 %copy-start.1 = (bf16[32,16,4096]{2,1,0:T(8,128)(2,1)}, bf16[32,16,4096]{2,1,0:T(8,128)(2,1)S(1)}, u32[]{:S(2)}) copy-start(bf16[32,16,4096]{2,1,0:T(8,128)(2,1)S(1)} %select_convert_fusion) | copy-start | bytes 12582916
  68.9 3.7 %copy-start.2 = (f32[32,1,16]{0,2,1:T(8,128)S(1)}, f32[32,1,16]{0,2,1:T(8,128)}, u32[]{:S(2)}) copy-start(f32[32,1,16]{0,2,1:T(8,128)} %param.9) | copy-start | bytes 6148
  68.9 13.3 %copy-start = (bf16[32,16,4096]{2,1,0:T(8,128)(2,1)S(1)}, bf16[32,16,4096]{2,1,0:T(8,128)(2,1)}, u32[]{:S(2)}) copy-start(bf16[32,16,4096]{2,1,0:T(8,128)(2,1)} %weight_hbm.1) | copy-start | bytes 12582916
  70.2 1.6 %collective-permute-start = (f32[520,128]{1,0:T(8,128)S(1)}, f32[520,128]{1,0:T(8,128)S(1)}, u32[]{:S(2)}, u32[]{:S(2)}) collective-permute-start(f32[520,128]{1,0:T(8,128)S(1)} %shard_map.77), channel_id=1, source_target_pairs={{0,1},{1,0},{2,3},{3,2},{4,5},{5,4},{6,7},{7,6},{8,9},{9,8},{10,11... | collective-permute-start | bytes 798728 | tf_op jit(solution)/shard_map/ppermute | solution.py:251
  71.8 8.7 %collective-permute-start.1 = (f32[520,128]{1,0:T(8,128)S(1)}, f32[520,128]{1,0:T(8,128)S(1)}, u32[]{:S(2)}, u32[]{:S(2)}) collective-permute-start(f32[520,128]{1,0:T(8,128)S(1)} %add.27), channel_id=1, source_target_pairs={{0,2},{1,3},{2,0},{3,1},{4,6},{5,7},{6,4},{7,5},{8,10},{9,11},{10,... | collective-permute-start | bytes 798728 | tf_op jit(solution)/shard_map/ppermute | solution.py:255
  80.6 1.6 %collective-permute-start.2 = (f32[520,128]{1,0:T(8,128)S(1)}, f32[520,128]{1,0:T(8,128)S(1)}, u32[]{:S(2)}, u32[]{:S(2)}) collective-permute-start(f32[520,128]{1,0:T(8,128)S(1)} %add.28.mine_ref), channel_id=1, source_target_pairs={{0,1},{1,0},{2,3},{3,2},{4,5},{5,4},{6,7},{7,6},{8,9},{9,8},{10,11... | collective-permute-start | bytes 798728 | tf_op jit(solution)/shard_map/ppermute | solution.py:257

commit v5 on v4

--- a/solution.py
+++ b/solution.py
@@ -296,7 +296,7 @@
 
 def apply_step(kv_weight, received):
     layers, rows, cols = kv_weight.shape
-    group = layers // 4
+    group = layers // 2
     shape = jax.ShapeDtypeStruct(kv_weight.shape, bf16)
     return pl.pallas_call(
         step_kernel,

time: 156 us -> 155 us (level)
  no operation moved by 1% of the time
where the time goes in v5:
time: 155 us; the launch traced here: 154 us
  blocking collectives  122 us (79%)
  Pallas kernels  16.4 us (11%)
  waiting for transfers between devices  9.66 us (6%)
  other arithmetic  4.53 us (3%)
    all_to_all x1, blocking collectives, on_device(): lax.all_to_all(new_momentum, 'dp', split_axis=0, concat_axis=0, tiled=True)  63.7 us
    all_to_all x1, blocking collectives, on_device(): lax.all_to_all(owned_update.reshape(layers, rows, shard_width + TILE), 'd...  58.3 us
    pallas_call x1, Pallas kernels, scaled_update(): pl.pallas_call(functools.partial(update_kernel, 0.2 * math.sqrt(max(LATEN...  10.4 us
    ppermute x1, waiting for transfers between devices, gram_sum(): mine = mine + lax.ppermute(mine, 'tensor', other_chip)  7.95 us
    convert_element_type x1, other arithmetic, on_device(): new_momentum = (live_mask * (momentum_decay * momentum.astype(f32) + grad...  4.43 us
    pallas_call x1, Pallas kernels, apply_step(): pl.pallas_call(step_kernel, grid=(layers // group,), out_shape=(shape, sh...  3.38 us
  transfers between devices with their start and end apart: 3, of which 3 were waited for; matrix products, arithmetic and copies ran while one was open for 0% of the time, Pallas kernels for 1%

profile of v5, /device:TPU:0, one launch (start us, length us, event | category | flops | bytes accessed | tf_op | source)
XLA Modules:
  0.0 154.4 jit_solution(2174055773342679784)
XLA Ops:
  0.7 4.4 %select_convert_fusion = bf16[32,16,4096]{2,1,0:T(8,128)(2,1)S(1)} fusion(bf16[32,16,4096]{2,1,0:T(8,128)(2,1)} %param.7, bf16[32,16,4096]{2,1,0:T(8,128)(2,1)} %param.6, s32[32]{0:T(128)} %param.8, s32[4096]{0:T(1024)S(1)} %get-tuple-element.23, s32[4096]{0:T(1024)S(1)} %get-tuple-element.24, s32[]{:T(128)S(6)} %mul.12, pred[4096]{0:T(1024)(128)(4,1)S(1)} %fusion.2), kind=kLoop, calls=%fused_computation | loop fusion | flops 18874368 | bytes 12619908 | tf_op jit(solution)/shard_map/convert_element_type | solution.py:330
  5.1 0.0 copy-start.1
  5.1 63.7 %all_to_all.10 = bf16[32,16,4096]{2,1,0:T(8,128)(2,1)S(1)} all-to-all(bf16[32,16,4096]{2,1,0:T(8,128)(2,1)S(1)} %select_convert_fusion), channel_id=1, replica_groups=mesh['dp'=32,'tensor'=4] {'dp'}, dimensions={0} | all-to-all | bytes 8388608 | tf_op jit(solution)/shard_map/all_to_all | solution.py:332
  68.9 0.0 copy-start.2
  68.9 0.0 copy-start
  68.9 1.3 shard_map.77
  70.2 0.0 copy-done.1
  70.2 0.1 collective-permute-start
  70.3 1.3 shard_map.76
  71.6 0.2 collective-permute-done
  71.8 0.7 collective-permute-start.1
  72.6 0.0 copy-done.2
  72.6 7.9 %collective-permute-done.1 = f32[520,128]{1,0:T(8,128)S(1)} collective-permute-done((f32[520,128]{1,0:T(8,128)S(1)}, f32[520,128]{1,0:T(8,128)S(1)}, u32[]{:S(2)}, u32[]{:S(2)}) %collective-permute-start.1) | collective-permute-done | bytes 266272 | tf_op jit(solution)/shard_map/ppermute | solution.py:255
  80.6 0.1 collective-permute-start.2
  80.7 1.5 collective-permute-done.2.other_ref
  82.2 0.0 copy-done
  82.2 10.4 %shard_map.78 = (bf16[512,4224]{1,0:T(8,128)(2,1)S(1)}, bf16[32,16,4096]{2,1,0:T(8,128)(2,1)S(1)}) custom-call(s32[1]{0:T(128)} %bitcast.core_ref, f32[520,128]{1,0:T(8,128)S(1)} %add.28.mine_ref, f32[520,128]{1,0:T(8,128)S(1)} %collective-permute-done.2.other_ref, f32[16,128]{1,0:T(8,128)S(1)} %pad.4.peak_ref, bf16[512,4096]{1,0:T(8,128)(2,1)S(1)} %bitcast.8, ...), custom_call_target="tpu_custom_call" | custom-call | flops 6710886400 | bytes 8388608 | tf_op jit(solution)/shard_map/pallas_call | solution.py:226
  92.6 58.3 %all_to_all.11.recv_ref = bf16[32,16,4224]{2,1,0:T(8,128)(2,1)S(1)} all-to-all(bf16[32,16,4224]{2,1,0:T(8,128)(2,1)S(1)} %bitcast.9), channel_id=1, replica_groups=mesh['dp'=32,'tensor'=4] {'dp'}, dimensions={0} | all-to-all | bytes 8650752 | tf_op jit(solution)/shard_map/all_to_all | solution.py:338
  150.9 3.4 %shard_map.79 = (bf16[32,16,4096]{2,1,0:T(8,128)(2,1)}, bf16[32,16,4096]{2,1,0:T(8,128)(2,1)}) custom-call(bf16[32,16,4096]{2,1,0:T(8,128)(2,1)S(1)} %get-tuple-element.19.weight_ref, bf16[32,16,4224]{2,1,0:T(8,128)(2,1)S(1)} %all_to_all.11.recv_ref), custom_call_target="tpu_custom_call" | custom-call | flops 8388608 | bytes 16777216 | tf_op jit(solution)/shard_map/pallas_call | solution.py:301
  (5 shorter events, 0.1 us)
Async XLA Ops:
  5.1 65.1 %copy-start.1 = (bf16[32,16,4096]{2,1,0:T(8,128)(2,1)}, bf16[32,16,4096]{2,1,0:T(8,128)(2,1)S(1)}, u32[]{:S(2)}) copy-start(bf16[32,16,4096]{2,1,0:T(8,128)(2,1)S(1)} %select_convert_fusion) | copy-start | bytes 12582916
  68.9 3.7 %copy-start.2 = (f32[32,1,16]{0,2,1:T(8,128)S(1)}, f32[32,1,16]{0,2,1:T(8,128)}, u32[]{:S(2)}) copy-start(f32[32,1,16]{0,2,1:T(8,128)} %param.9) | copy-start | bytes 6148
  68.9 13.3 %copy-start = (bf16[32,16,4096]{2,1,0:T(8,128)(2,1)S(1)}, bf16[32,16,4096]{2,1,0:T(8,128)(2,1)}, u32[]{:S(2)}) copy-start(bf16[32,16,4096]{2,1,0:T(8,128)(2,1)} %weight_hbm.1) | copy-start | bytes 12582916
  70.2 1.6 %collective-permute-start = (f32[520,128]{1,0:T(8,128)S(1)}, f32[520,128]{1,0:T(8,128)S(1)}, u32[]{:S(2)}, u32[]{:S(2)}) collective-permute-start(f32[520,128]{1,0:T(8,128)S(1)} %shard_map.77), channel_id=1, source_target_pairs={{0,1},{1,0},{2,3},{3,2},{4,5},{5,4},{6,7},{7,6},{8,9},{9,8},{10,11... | collective-permute-start | bytes 798728 | tf_op jit(solution)/shard_map/ppermute | solution.py:251
  71.8 8.7 %collective-permute-start.1 = (f32[520,128]{1,0:T(8,128)S(1)}, f32[520,128]{1,0:T(8,128)S(1)}, u32[]{:S(2)}, u32[]{:S(2)}) collective-permute-start(f32[520,128]{1,0:T(8,128)S(1)} %add.27), channel_id=1, source_target_pairs={{0,2},{1,3},{2,0},{3,1},{4,6},{5,7},{6,4},{7,5},{8,10},{9,11},{10,... | collective-permute-start | bytes 798728 | tf_op jit(solution)/shard_map/ppermute | solution.py:255
  80.6 1.6 %collective-permute-start.2 = (f32[520,128]{1,0:T(8,128)S(1)}, f32[520,128]{1,0:T(8,128)S(1)}, u32[]{:S(2)}, u32[]{:S(2)}) collective-permute-start(f32[520,128]{1,0:T(8,128)S(1)} %add.28.mine_ref), channel_id=1, source_target_pairs={{0,1},{1,0},{2,3},{3,2},{4,5},{5,4},{6,7},{7,6},{8,9},{9,8},{10,11... | collective-permute-start | bytes 798728 | tf_op jit(solution)/shard_map/ppermute | solution.py:257
